TPU v7x, 256 devices: a whole 4x4x8 slice. The times are simulated.
256 devices in a mesh: member: 16 (over y_lo, x, core), fsdp: 16 (over y_hi, z).
Axes of the slice: x: 4, y: 4 (y_hi: 2, y_lo: 2; y = y_hi * 2 + y_lo), z: 8, core: 2. Of those that a mesh axis runs over, the one named last changes fastest.
Arguments:
- analysis: float32 [16, 12, 16, 16, 1024], P('member', None, 'fsdp'), may hold values from -6 to 6
- owner: int32 [1], replicated, may hold values from 0 to 15
- noise: bfloat16 [128, 12, 16, 16, 1024], P('member', None, 'fsdp'), may hold values from -4 to 4
- depth_weight: float32 [3, 3, 1024], replicated, may hold values from -2 to 2
- depth_bias: float32 [1024], replicated, may hold values from -3 to 3
- norm_gain: float32 [1024], replicated, may hold values from 0.1 to 1.9
- up_weight: bfloat16 [1024, 2048], P('fsdp'), may hold values from -0.1875 to 0.1875
- up_bias: float32 [2048], replicated, may hold values from -3 to 3
- down_weight: bfloat16 [2048, 1024], P('fsdp'), may hold values from -0.125 to 0.125
- down_bias: float32 [1024], replicated, may hold values from -3 to 3
Outputs:
- block_out: bfloat16 [128, 12, 16, 16, 1024], P('member', None, 'fsdp')
All inputs are finite; a program needn't handle non-finite values.
Results may differ from a plain program's by a relative error of at most 0.0054.
Values may be sent and summed in bfloat16 or wider, within the bound.
A program may use at most 128 MiB of HBM per device.

v0:
```python
import jax
import jax.numpy as jnp
import numpy as np
from jax import lax
from jax.sharding import PartitionSpec as P

up_table = np.array([(f + 4) % 12 for f in range(12)], dtype=np.int32)
down_table = np.array([(f + 8) % 12 for f in range(12)], dtype=np.int32)
left_table = np.array([4 * (f // 4) + (f + 3) % 4 for f in range(12)], dtype=np.int32)
right_table = np.array([4 * (f // 4) + (f + 1) % 4 for f in range(12)], dtype=np.int32)


def from_root(shard, axis, root):
    mine = lax.axis_index(axis) == root
    return lax.psum(jnp.where(mine, shard, jnp.zeros_like(shard)), axis)


def padded_2(cells, sides, width):
    for axis, dim in sides:
        count = lax.axis_size(axis)
        head = lax.slice_in_dim(cells, 0, width, axis=dim)
        tail = lax.slice_in_dim(cells, cells.shape[dim] - width, cells.shape[dim], axis=dim)
        cells = jnp.concatenate(
            [
                lax.ppermute(tail, axis, [(i, (i + 1) % count) for i in range(count)]),
                cells,
                lax.ppermute(head, axis, [((i + 1) % count, i) for i in range(count)]),
            ],
            axis=dim,
        )
    return cells


def shards(
    analysis,
    owner,
    noise,
    depth_weight,
    depth_bias,
    norm_gain,
    up_weight,
    up_bias,
    down_weight,
    down_bias,
):
    state = from_root(analysis, "member", owner[0])
    start = (state + noise.astype(jnp.float32)).astype(jnp.bfloat16)
    row_count = start.shape[2]
    side = start.shape[3]
    width = start.shape[4]
    extended = padded_2(start, (("fsdp", 2),), 1)
    lower_rim = extended[:, :, 0:1]
    upper_rim = extended[:, :, row_count + 1 : row_count + 2]
    position = lax.axis_index("fsdp")
    lower_rim = jnp.where(position == 0, lower_rim[:, up_table], lower_rim)
    upper_rim = jnp.where(
        position == lax.axis_size("fsdp") - 1, upper_rim[:, down_table], upper_rim
    )
    rows = jnp.concatenate([lower_rim, start, upper_rim], axis=2)
    padded = jnp.concatenate(
        [rows[:, left_table][:, :, :, side - 1 : side], rows, rows[:, right_table][:, :, :, 0:1]],
        axis=3,
    )
    conv = jnp.zeros(start.shape, jnp.float32) + depth_bias
    for i in range(3):
        for j in range(3):
            conv = conv + depth_weight[i, j] * padded[:, :, i : i + row_count, j : j + side].astype(
                jnp.float32
            )
    mean = jnp.mean(conv, axis=-1, keepdims=True)
    var = jnp.mean(jnp.square(conv - mean), axis=-1, keepdims=True)
    normed = ((conv - mean) * lax.rsqrt(var + 1e-06) * norm_gain).astype(jnp.bfloat16)
    flat = normed.reshape(-1, width)
    columns = flat
    upper = jnp.zeros((flat.shape[0], up_weight.shape[1]), jnp.float32) + jnp.dot(
        columns,
        lax.all_gather(up_weight, "fsdp", axis=0, tiled=True),
        preferred_element_type=jnp.float32,
    )
    hidden = jax.nn.gelu(upper + up_bias, approximate=True).astype(jnp.bfloat16)
    columns = hidden
    lower = jnp.zeros((flat.shape[0], width), jnp.float32) + jnp.dot(
        columns,
        lax.all_gather(down_weight, "fsdp", axis=0, tiled=True),
        preferred_element_type=jnp.float32,
    )
    result = start.reshape(-1, width).astype(jnp.float32) + lower + down_bias
    return result.astype(jnp.bfloat16).reshape(start.shape)


def solution(mesh):
    placed = (
        P("member", None, "fsdp", None, None),
        P(),
        P("member", None, "fsdp", None, None),
        P(),
        P(),
        P(),
        P("fsdp", None),
        P(),
        P("fsdp", None),
        P(),
    )
    return jax.shard_map(
        shards,
        mesh=mesh,
        in_specs=placed,
        out_specs=P("member", None, "fsdp", None, None),
        check_vma=False,
    )
```

profile of v0, /device:TPU:1, one launch (start us, length us, event | category | flops | bytes accessed | tf_op | source)
XLA Modules:
  0.0 349.1 jit_solution(12348842522407410237)
XLA Ops:
  8.1 1.0 select_bitcast_fusion
  9.7 129.4 %all-reduce.2.cloned.1.call-done = f32[12,16,1024]{2,1,0:T(8,128)} async-done(((f32[12,16,1024]{2,1,0:T(8,128)}), f32[12,16,1024]{2,1,0:T(8,128)}) %all-reduce.2.cloned.1.call-update) | async-done | bytes 786448 | tf_op jit(solution)/shard_map/psum | solution.py:15
  139.1 3.0 add_convert_fusion
  142.1 1.4 collective-permute-start
  143.5 4.0 %collective-permute-start.1 = (bf16[8,12,1,16,1024]{4,3,0,1,2:T(8,128)(2,1)S(1)}, bf16[8,12,1,16,1024]{4,3,0,1,2:T(8,128)(2,1)}, u32[]{:S(2)}, u32[]{:S(2)}) collective-permute-start(bf16[8,12,1,16,1024]{4,3,0,1,2:T(8,128)(2,1)S(1)} %add_convert_fusion), channel_id=1, source_target_pairs={{1,0},{2,1},{3,2},{4,3},{5,4},{6,5},{7,6},{8,7},{9,8},{10,9},{11,1... | collective-permute-start | bytes 9437192 | tf_op jit(solution)/shard_map/ppermute | solution.py:27
  147.6 3.4 copy.35
  151.0 66.4 %collective-permute-done = bf16[8,12,1,16,1024]{4,3,0,1,2:T(8,128)(2,1)} collective-permute-done((bf16[8,12,1,16,1024]{4,3,0,1,2:T(8,128)(2,1)S(1)}, bf16[8,12,1,16,1024]{4,3,0,1,2:T(8,128)(2,1)}, u32[]{:S(2)}, u32[]{:S(2)}) %collective-permute-start) | collective-permute-done | bytes 3145760 | tf_op jit(solution)/shard_map/ppermute | solution.py:25
  217.4 4.1 %copy.36 = bf16[8,12,16,1024]{3,2,1,0:T(8,128)(2,1)} copy(bf16[8,12,16,1024]{3,2,0,1:T(8,128)(2,1)} %bitcast.4) | data formatting | bytes 6291456 | tf_op jit(solution)/shard_map/ppermute | solution.py:25
  221.5 4.4 %gather_fusion = bf16[12,8,16,1024]{3,2,1,0:T(8,128)(2,1)} fusion(bf16[8,12,16,1024]{3,2,1,0:T(8,128)(2,1)} %copy.36, s32[1024]{0:T(1024)S(1)} %pad_clamp_fusion.3), kind=kCustom, calls=%fused_computation | custom fusion | bytes 6291504 | tf_op jit(solution)/shard_map/gather | solution.py:55
  225.9 4.4 %gather_fusion.1 = bf16[12,8,16,1024]{3,2,1,0:T(8,128)(2,1)} fusion(bf16[8,12,16,1024]{3,2,0,1:T(8,128)(2,1)} %bitcast.7, s32[1024]{0:T(1024)S(1)} %pad_clamp_fusion.2), kind=kCustom, calls=%fused_computation.1 | custom fusion | bytes 6291504 | tf_op jit(solution)/shard_map/gather | solution.py:57
  230.3 4.0 %bitcast_select_fusion.1 = bf16[8,12,1,16,1024]{4,3,0,1,2:T(8,128)(2,1)} fusion(bf16[8,12,1,16,1024]{4,3,0,1,2:T(8,128)(2,1)} %collective-permute-done, bf16[12,8,16,1024]{3,2,1,0:T(8,128)(2,1)} %gather_fusion, pred[]{:T(512)S(6)} %eq.10), kind=kLoop, calls=%fused_computation.30 | loop fusion | flops 1572864 | bytes 9437185 | tf_op jit(solution)/shard_map/jit(_where)/select_n | solution.py:55
  234.3 4.0 %bitcast_select_fusion = bf16[8,12,1,16,1024]{4,3,0,1,2:T(8,128)(2,1)} fusion(bf16[8,12,1,16,1024]{4,3,0,1,2:T(8,128)(2,1)} %collective-permute-done.1, bf16[12,8,16,1024]{3,2,1,0:T(8,128)(2,1)S(1)} %copy-done, pred[]{:T(512)S(6)} %eq.11), kind=kLoop, calls=%fused_computation.29 | loop fusion | flops 1572864 | bytes 9437185 | tf_op jit(solution)/shard_map/jit(_where)/select_n | solution.py:56
  238.3 6.9 %pad_maximum_fusion = bf16[8,12,3,16,1024]{4,3,0,1,2:T(8,128)(2,1)} fusion(bf16[8,12,1,16,1024]{4,3,0,1,2:T(8,128)(2,1)} %bitcast_select_fusion, bf16[8,12,1,16,1024]{4,3,0,1,2:T(8,128)(2,1)S(1)} %add_convert_fusion, bf16[8,12,1,16,1024]{4,3,0,1,2:T(8,128)(2,1)} %bitcast_select_fusion.1), kind=kLoop, calls=%fused_computation.13 | loop fusion | flops 9437184 | bytes 18874368 | tf_op jit(solution)/shard_map/concatenate | solution.py:59
  245.2 9.8 %copy.37 = bf16[8,12,3,16,1024]{4,3,2,1,0:T(8,128)(2,1)} copy(bf16[8,12,3,16,1024]{4,3,0,1,2:T(8,128)(2,1)} %pad_maximum_fusion) | data formatting | bytes 18874368 | tf_op jit(solution)/shard_map/concatenate | solution.py:59
  255.0 9.4 %gather_fusion.2 = bf16[12,8,3,16,1024]{4,3,2,1,0:T(8,128)(2,1)} fusion(bf16[8,12,3,16,1024]{4,3,2,1,0:T(8,128)(2,1)} %copy.37, s32[1024]{0:T(1024)S(1)} %pad_clamp_fusion.1), kind=kCustom, calls=%fused_computation.2 | custom fusion | bytes 18874416 | tf_op jit(solution)/shard_map/gather | solution.py:61
  264.4 9.6 %copy.47 = bf16[12,8,3,16,1024]{4,3,1,0,2:T(8,128)(2,1)} copy(bf16[12,8,3,16,1024]{4,3,2,1,0:T(8,128)(2,1)} %gather_fusion.2) | data formatting | bytes 18874368 | tf_op jit(solution)/shard_map/gather | solution.py:61
  274.0 4.8 %slice.82 = bf16[8,12,3,1,1024]{4,3,0,1,2:T(2,128)(2,1)} slice(bf16[8,12,3,16,1024]{4,3,0,1,2:T(8,128)(2,1)} %bitcast.51), slice={[0:8], [0:12], [0:3], [15:16], [0:1024]} | slice | bytes 1179648 | tf_op jit(solution)/shard_map/slice | solution.py:61
  278.8 9.4 %gather_fusion.3 = bf16[12,8,3,16,1024]{4,3,2,1,0:T(8,128)(2,1)} fusion(bf16[8,12,3,16,1024]{4,3,2,1,0:T(8,128)(2,1)} %copy.37, s32[1024]{0:T(1024)S(1)} %pad_clamp_fusion), kind=kCustom, calls=%fused_computation.3 | custom fusion | bytes 18874416 | tf_op jit(solution)/shard_map/gather | solution.py:61
  288.2 9.6 %copy.46 = bf16[12,8,3,16,1024]{4,3,1,0,2:T(8,128)(2,1)} copy(bf16[12,8,3,16,1024]{4,3,2,1,0:T(8,128)(2,1)} %gather_fusion.3) | data formatting | bytes 18874368 | tf_op jit(solution)/shard_map/gather | solution.py:61
  297.9 3.6 %slice.83 = bf16[8,12,3,1,1024]{4,3,0,1,2:T(2,128)(2,1)S(1)} slice(bf16[8,12,3,16,1024]{4,3,0,1,2:T(8,128)(2,1)} %bitcast.52), slice={[0:8], [0:12], [0:3], [0:1], [0:1024]} | slice | bytes 1179648 | tf_op jit(solution)/shard_map/slice | solution.py:61
  301.5 18.1 %fusion.10 = (f32[8,12,16]{2,0,1:T(8,128)S(1)}, f32[8,12,1,16,1024]{4,3,0,1,2:T(8,128)S(1)}) fusion(bf16[8,12,3,1,1024]{4,3,0,1,2:T(2,128)(2,1)S(1)} %slice.83, bf16[8,12,1,16,1024]{4,3,0,1,2:T(8,128)(2,1)} %bitcast_select_fusion, bf16[8,12,1,16,1024]{4,3,0,1,2:T(8,128)(2,1)S(1)} %add_convert_fusion, bf16[8,12,1,16,1024]{4,3,0,1,2:T(8,128)(2,1)} %bitcast_select_fusion.1, ...), kind=kLoop, calls=%fused_computation.38 | loop fusion | flops 110098944 | bytes 16955392 | tf_op jit(solution)/shard_map/reduce_sum | solution.py:70
  319.6 0.8 multiply_reduce_fusion
  320.4 1.2 multiply_convert_fusion
  322.0 19.6 %fusion.9 = bf16[1536,1024]{1,0:T(8,128)(2,1)} fusion(f32[8,12,1,16,1024]{4,3,1,0,2:T(8,128)} %copy.35, bf16[2048,1024]{1,0:T(8,128)(2,1)} %all-gather.5.cloned.1.call-done, f32[1024]{0:T(1024)S(1)} %copy-done.9, bf16[1536,1024]{1,0:T(8,128)(2,1)S(1)} %bitcast.53, bf16[1024,2048]{1,0:T(8,128)(2,1)} %all-gather.3.cloned.1.call-done, f32[2048]{0:T(1024)S(1)} %copy-done.8), kind=kOutput, calls=%fused_computation.18 | convolution fusion | flops 12921077760 | bytes 20983808 | tf_op jit(solution)/shard_map/dot_general | solution.py:82
  (37 shorter events, 1.2 us)
Async XLA Ops:
  7.4 140.1 %copy-start.7 = (s32[12]{0:T(128)S(1)}, s32[12]{0:T(128)}, u32[]{:S(2)}) copy-start(s32[12]{0:T(128)} %constant.51) | copy-start | bytes 148
  7.4 140.1 %copy-start.6 = (s32[12]{0:T(128)S(1)}, s32[12]{0:T(128)}, u32[]{:S(2)}) copy-start(s32[12]{0:T(128)} %constant.52) | copy-start | bytes 148
  7.4 140.2 %copy-start.5 = (s32[12]{0:T(128)S(1)}, s32[12]{0:T(128)}, u32[]{:S(2)}) copy-start(s32[12]{0:T(128)} %constant.53) | copy-start | bytes 148
  7.4 140.2 %copy-start.4 = (s32[12]{0:T(128)S(1)}, s32[12]{0:T(128)}, u32[]{:S(2)}) copy-start(s32[12]{0:T(128)} %constant.54) | copy-start | bytes 148
  7.4 140.2 %copy-start.1 = (f32[3,3,1024]{2,1,0:T(4,128)S(1)}, f32[3,3,1024]{2,1,0:T(4,128)}, u32[]{:S(2)}) copy-start(f32[3,3,1024]{2,1,0:T(4,128)} %param.21) | copy-start | bytes 110596
  7.4 131.7 %all-reduce.2.cloned.1.call-start = ((), (), s32[]{:S(2)}) async-start(), calls=%async_computation | async-start | bytes 1572864 | tf_op jit(solution)/shard_map/psum | solution.py:15
  9.1 312.9 %all-gather.3.cloned.1.call-start = ((), (), s32[]{:S(2)}) async-start(), calls=%async_computation.1 | async-start | bytes 4456448 | tf_op jit(solution)/shard_map/all_gather | solution.py:77
  9.7 312.3 %all-gather.5.cloned.1.call-start = ((), (), s32[]{:S(2)}) async-start(), calls=%async_computation.2 | async-start | bytes 4456448 | tf_op jit(solution)/shard_map/all_gather | solution.py:84
  142.1 75.3 %collective-permute-start = (bf16[8,12,1,16,1024]{4,3,0,1,2:T(8,128)(2,1)S(1)}, bf16[8,12,1,16,1024]{4,3,0,1,2:T(8,128)(2,1)}, u32[]{:S(2)}, u32[]{:S(2)}) collective-permute-start(bf16[8,12,1,16,1024]{4,3,0,1,2:T(8,128)(2,1)S(1)} %add_convert_fusion), channel_id=1, source_target_pairs={{0,1},{1,2},{2,3},{3,4},{4,5},{5,6},{6,7},{7,8},{8,9},{9,10},{10,1... | collective-permute-start | bytes 9437192 | tf_op jit(solution)/shard_map/ppermute | solution.py:25
  143.5 82.4 %collective-permute-start.1 = (bf16[8,12,1,16,1024]{4,3,0,1,2:T(8,128)(2,1)S(1)}, bf16[8,12,1,16,1024]{4,3,0,1,2:T(8,128)(2,1)}, u32[]{:S(2)}, u32[]{:S(2)}) collective-permute-start(bf16[8,12,1,16,1024]{4,3,0,1,2:T(8,128)(2,1)S(1)} %add_convert_fusion), channel_id=1, source_target_pairs={{1,0},{2,1},{3,2},{4,3},{5,4},{6,5},{7,6},{8,7},{9,8},{10,9},{11,1... | collective-permute-start | bytes 9437192 | tf_op jit(solution)/shard_map/ppermute | solution.py:27
  230.3 4.0 %copy-start = (bf16[12,8,16,1024]{3,2,1,0:T(8,128)(2,1)S(1)}, bf16[12,8,16,1024]{3,2,1,0:T(8,128)(2,1)}, u32[]{:S(2)}) copy-start(bf16[12,8,16,1024]{3,2,1,0:T(8,128)(2,1)} %gather_fusion.1) | copy-start | bytes 9437188
  288.2 13.2 %copy-start.2 = (f32[1024]{0:T(1024)S(1)}, f32[1024]{0:T(1024)}, u32[]{:S(2)}) copy-start(f32[1024]{0:T(1024)} %param.22) | copy-start | bytes 12292
  319.5 0.9 copy-start.3
  320.4 1.6 copy-start.8
  320.4 1.6 copy-start.9
Sparse Core Ops, SparseCore 0:
  10.8 128.2 all-reduce.1
Sparse Core Ops, SparseCore 1:
  12.5 102.2 all-gather.2
  147.6 146.2 all-gather.4
where the time goes:
time: 350 us; the launch traced here: 349 us
  waiting for transfers between devices  196 us (56%)
  local copies, waits for them, and re-layouts  72.9 us (21%)
  other arithmetic  39 us (11%)
  matrix products  19.6 us (6%)
  between operations  15.8 us (5%)
  starting transfers between devices  5.44 us (2%)
    psum x1, waiting for transfers between devices, from_root(): return lax.psum(jnp.where(mine, shard, jnp.zeros_like(shard)), axis)  129 us
    ppermute x1, waiting for transfers between devices, padded_2(): lax.ppermute(tail, axis, [(i, (i + 1) % count) for i in range(count)])  66.4 us
    dot_general x1, matrix products, shards(): jnp.dot(columns, lax.all_gather(down_weight, 'fsdp', axis=0, tiled=True),...  19.6 us
    gather x2, local copies, waits for them, and re-layouts, shards(): rows[:, right_table][:, :, :, 0:1]  19.1 us
    gather x2, local copies, waits for them, and re-layouts, shards(): rows[:, left_table][:, :, :, side - 1:side]  18.9 us
    reduce_sum x1, other arithmetic, shards(): mean = jnp.mean(conv, axis=-1, keepdims=True)  18.1 us
    concatenate x1, local copies, waits for them, and re-layouts, shards(): rows = jnp.concatenate([lower_rim, start, upper_rim], axis=2)  9.79 us
  transfers between devices with their start and end apart: 5, of which 2 were waited for; matrix products, arithmetic and copies ran while one was open for 32% of the time, Pallas kernels for 0%

commit v1 on v0

v1 whole, which is shorter than its diff:
```python
import functools

import jax
import jax.numpy as jnp
from jax import lax
from jax.experimental import pallas as pl
from jax.experimental.pallas import tpu as pltpu
from jax.sharding import PartitionSpec as P

GROUPS = 3
MEM = 8
UNITS = GROUPS * MEM
RING = 64
C = 1024
HID = 2048
PER_BATCH = 4
BATCHES = UNITS // PER_BATCH
ROWS = PER_BATCH * RING
HALF = C // 2
SLICE = GROUPS * RING // 4
UP_W = HID // 8
DN_W = C // 8
MESH = pl.DeviceIdType.MESH


def gelu(v):
    return 0.5 * v * (1.0 + jnp.tanh(0.7978845608028654 * (v + 0.044715 * (v * v * v))))


def kernel(
    owner_ref, analysis, noise, dw, db, gain, wu, ub, wd, bd, out,
    own, halo_up, halo_dn, normed, wup, wdn, st, pair, pick, xs_buf, ys_buf, conv, hid,
    halo_s, halo_r, zs, zr, ys, yr, xs, xr, cs, cr, a_s, a_r, local,
):
    m = lax.axis_index("member")
    p = lax.axis_index("fsdp")
    core = lax.rem(m, 2)
    x = lax.rem(lax.div(m, 2), 4)
    yl = lax.div(m, 8)
    yh = lax.div(p, 8)
    z = lax.rem(p, 8)
    y = yh * 2 + yl
    sib_core = 1 - core

    def dev(mm, pp):
        return {"member": mm, "fsdp": pp}

    def zdev(k):
        return dev(m, yh * 8 + lax.rem(z + k, 8))

    def xdev(k):
        return dev(yl * 8 + lax.rem(x + k, 4) * 2 + core, p)

    def ypos(k):
        q = lax.rem(y + k, 4)
        return lax.div(q, 2), lax.rem(q, 2)

    def ydev(k):
        h, l = ypos(k)
        return dev(l * 8 + x * 2 + core, h * 8 + z)

    sib = dev(yl * 8 + x * 2 + sib_core, p)
    nxt = dev(m, lax.rem(p + 1, 16))
    prv = dev(m, lax.rem(p + 15, 16))

    def rc(src, dst, s, r, d):
        return pltpu.make_async_remote_copy(
            src_ref=src, dst_ref=dst, send_sem=s, recv_sem=r, device_id=d, device_id_type=MESH
        )

    barrier = pltpu.get_barrier_semaphore()
    partners = [zdev(k) for k in range(1, 8)] + [nxt, prv] + [xdev(k) for k in (1, 2, 3)]
    partners += [ydev(1), ydev(3), sib]
    for d in partners:
        pl.semaphore_signal(barrier, inc=1, device_id=d, device_id_type=MESH)
    pl.semaphore_wait(barrier, len(partners))

    waits = []

    def send(desc):
        desc.start()
        waits.append(desc)

    def ch(cc):
        return pl.ds(pl.multiple_of(cc * HALF, HALF), HALF)

    def up_cols(xx, cc):
        return pl.ds(pl.multiple_of((xx * 2 + cc) * UP_W, UP_W), UP_W)

    def dn_cols(xx, cc):
        return pl.ds(pl.multiple_of((xx * 2 + cc) * DN_W, DN_W), DN_W)

    def srows(xx):
        return pl.ds(pl.multiple_of(xx * SLICE, SLICE), SLICE)

    send(rc(analysis.at[:, ch(sib_core)], pair.at[core], a_s.at[0], a_r.at[0], sib))
    c_pair = pltpu.make_async_copy(analysis.at[:, ch(core)], pair.at[core], local.at[0])
    c_pair.start()

    up_own, dn_own = up_cols(x, core), dn_cols(x, core)
    for k in range(1, 8):
        send(rc(wu.at[yl, :, up_own], wup.at[yh, z, yl, :, up_own], zs.at[0, k - 1], zr.at[0, k - 1], zdev(k)))
    for k in range(1, 8):
        send(rc(wd.at[yl, :, dn_own], wdn.at[yh, z, yl, :, dn_own], zs.at[1, k - 1], zr.at[1, k - 1], zdev(k)))
    c_up = pltpu.make_async_copy(wu.at[yl, :, up_own], wup.at[yh, z, yl, :, up_own], local.at[1])
    c_dn = pltpu.make_async_copy(wd.at[yl, :, dn_own], wdn.at[yh, z, yl, :, dn_own], local.at[2])
    c_own = pltpu.make_async_copy(noise, own, local.at[3])
    c_up.start()
    c_dn.start()
    c_own.start()

    first = p == 0
    last = p == 15

    def halo(u):
        g, mm = lax.div(u, MEM), lax.rem(u, MEM)
        g_up = jnp.where(last, lax.rem(g + 1, 3), g)
        g_dn = jnp.where(first, lax.rem(g + 2, 3), g)
        return (
            rc(noise.at[mm, g_up], halo_up.at[u], halo_s.at[0, u], halo_r.at[0, u], nxt),
            rc(noise.at[mm, g_dn], halo_dn.at[u], halo_s.at[1, u], halo_r.at[1, u], prv),
        )

    def start_halo(u, carry):
        a, b = halo(u)
        a.start()
        b.start()
        return carry

    lax.fori_loop(0, UNITS, start_halo, 0)

    owner = owner_ref[0]
    c_pair.wait()
    rc(pair.at[core], pair.at[sib_core], a_s.at[0], a_r.at[0], sib).wait_recv()
    pick[...] = pair[lax.rem(owner, 2)]
    for k in (1, 2, 3):
        xx = lax.rem(x + k, 4)
        send(rc(pick.at[srows(xx)], xs_buf.at[x], a_s.at[k], a_r.at[k], xdev(k)))
    xs_buf[x] = pick[srows(x)]
    for k in (1, 2, 3):
        rc(xs_buf.at[x], xs_buf.at[lax.rem(x + 4 - k, 4)], a_s.at[k], a_r.at[k], xdev(k)).wait_recv()
    ys_buf[yl] = xs_buf[lax.rem(lax.div(owner, 2), 4)]
    partner = dev((1 - yl) * 8 + x * 2 + core, p)
    send(rc(ys_buf.at[yl], ys_buf.at[yl], a_s.at[4], a_r.at[4], partner))
    rc(ys_buf.at[yl], ys_buf.at[1 - yl], a_s.at[4], a_r.at[4], partner).wait_recv()
    st[1, srows(x), ch(core)] = ys_buf[lax.div(owner, 8)]
    mine = st.at[1, srows(x), ch(core)]
    send(rc(mine, st.at[0, srows(x), ch(core)], a_s.at[5], a_r.at[5], nxt))
    send(rc(mine, st.at[2, srows(x), ch(core)], a_s.at[6], a_r.at[6], prv))

    def spread(row):
        here = st.at[row, srows(x), ch(core)]
        for k in (1, 2, 3):
            i = 7 + row * 3 + k - 1
            send(rc(here, here, a_s.at[i], a_r.at[i], xdev(k)))

    spread(1)

    c_up.wait()
    c_dn.wait()
    for k in range(1, 8):
        zz = lax.rem(z + 8 - k, 8)
        rc(wu.at[yl, :, up_own], wup.at[yh, zz, yl, :, up_own], zs.at[0, k - 1], zr.at[0, k - 1], zdev(k)).wait_recv()
        rc(wd.at[yl, :, dn_own], wdn.at[yh, zz, yl, :, dn_own], zs.at[1, k - 1], zr.at[1, k - 1], zdev(k)).wait_recv()

    def up_y(k):
        h, l = ypos(k)
        return wup.at[h, :, l, :, up_own]

    def dn_y(k):
        h, l = ypos(k)
        return wdn.at[h, :, l, :, dn_own]

    send(rc(up_y(0), up_y(0), ys.at[0], yr.at[0], ydev(1)))
    send(rc(up_y(0), up_y(0), ys.at[1], yr.at[1], ydev(3)))
    send(rc(dn_y(0), dn_y(0), ys.at[2], yr.at[2], ydev(1)))
    send(rc(dn_y(0), dn_y(0), ys.at[3], yr.at[3], ydev(3)))

    rc(mine, st.at[0, srows(x), ch(core)], a_s.at[5], a_r.at[5], nxt).wait_recv()
    spread(0)
    rc(mine, st.at[2, srows(x), ch(core)], a_s.at[6], a_r.at[6], prv).wait_recv()
    spread(2)

    rc(up_y(0), up_y(3), ys.at[0], yr.at[0], ydev(1)).wait_recv()
    send(rc(up_y(3), up_y(3), ys.at[4], yr.at[4], ydev(1)))
    rc(dn_y(0), dn_y(1), ys.at[3], yr.at[3], ydev(3)).wait_recv()
    send(rc(dn_y(1), dn_y(1), ys.at[5], yr.at[5], ydev(3)))

    def state_half(row, cc):
        return st.at[row, :, ch(cc)]

    for row in range(3):
        for k in (1, 2, 3):
            i = 7 + row * 3 + k - 1
            there = st.at[row, srows(lax.rem(x + 4 - k, 4)), ch(core)]
            rc(there, there, a_s.at[i], a_r.at[i], xdev(k)).wait_recv()
        send(rc(state_half(row, core), state_half(row, core), a_s.at[16 + row], a_r.at[16 + row], sib))

    def up_x(k, cc=core):
        return wup.at[:, :, :, :, up_cols(lax.rem(x + k, 4), cc)]

    def dn_x(k, cc=core):
        return wdn.at[:, :, :, :, dn_cols(lax.rem(x + k, 4), cc)]

    rc(up_y(0), up_y(1), ys.at[1], yr.at[1], ydev(3)).wait_recv()
    rc(up_y(0), up_y(2), ys.at[4], yr.at[4], ydev(1)).wait_recv()
    send(rc(up_x(0), up_x(0), xs.at[0], xr.at[0], xdev(1)))
    send(rc(up_x(0), up_x(0), xs.at[1], xr.at[1], xdev(3)))
    rc(dn_y(0), dn_y(3), ys.at[2], yr.at[2], ydev(1)).wait_recv()
    rc(dn_y(0), dn_y(2), ys.at[5], yr.at[5], ydev(3)).wait_recv()
    send(rc(dn_x(0), dn_x(0), xs.at[2], xr.at[2], xdev(1)))
    send(rc(dn_x(0), dn_x(0), xs.at[3], xr.at[3], xdev(3)))
    send(rc(up_x(0), up_x(0), cs.at[0, 0], cr.at[0, 0], sib))
    send(rc(dn_x(0), dn_x(0), cs.at[1, 0], cr.at[1, 0], sib))

    for row in range(3):
        rc(state_half(row, core), state_half(row, sib_core), a_s.at[16 + row], a_r.at[16 + row], sib).wait_recv()
    c_own.wait()

    def cells(u, carry):
        g, mm = lax.div(u, MEM), lax.rem(u, MEM)
        a, b = halo(u)
        a.wait_recv()
        b.wait_recv()
        g0 = pl.multiple_of(jnp.where(first, lax.rem(g + 1, 3), g) * RING, RING)
        g1 = pl.multiple_of(g * RING, RING)
        g2 = pl.multiple_of(jnp.where(last, lax.rem(g + 2, 3), g) * RING, RING)
        total = jnp.zeros((RING, 128), jnp.float32)
        for lane in range(C // 128):
            cols = pl.ds(lane * 128, 128)
            r0 = (st[0, pl.ds(g0, RING), cols] + halo_up[u, :, cols].astype(jnp.float32)).astype(jnp.bfloat16)
            r1 = (st[1, pl.ds(g1, RING), cols] + own[mm, g, :, cols].astype(jnp.float32)).astype(jnp.bfloat16)
            r2 = (st[2, pl.ds(g2, RING), cols] + halo_dn[u, :, cols].astype(jnp.float32)).astype(jnp.bfloat16)
            out[mm, g, :, cols] = r1
            rows = [r.astype(jnp.float32) for r in (r0, r1, r2)]
            parts = []
            for j in range(3):
                acc = rows[0] * dw[pl.ds(j, 1), cols]
                acc = acc + rows[1] * dw[pl.ds(3 + j, 1), cols]
                acc = acc + rows[2] * dw[pl.ds(6 + j, 1), cols]
                parts.append(acc)
            v = parts[1] + db[:, cols] + pltpu.roll(parts[0], 1, 0) + pltpu.roll(parts[2], RING - 1, 0)
            conv[:, cols] = v
            total = total + v
        mean = jnp.sum(total, axis=1, keepdims=True) * (1.0 / C)
        square = jnp.zeros((RING, 128), jnp.float32)
        for lane in range(C // 128):
            cols = pl.ds(lane * 128, 128)
            v = conv[:, cols] - mean
            square = square + v * v
        var = jnp.sum(square, axis=1, keepdims=True) * (1.0 / C)
        inv = lax.rsqrt(var + 1e-06)
        for lane in range(C // 128):
            cols = pl.ds(lane * 128, 128)
            v = (conv[:, cols] - mean) * inv * gain[:, cols]
            normed[pl.ds(pl.multiple_of(u * RING, RING), RING), cols] = v.astype(jnp.bfloat16)
        return carry

    def mlp(b, carry):
        rows = pl.ds(pl.multiple_of(b * ROWS, ROWS), ROWS)
        left = normed[rows, :]
        for n in range(4):
            cols = pl.ds(n * 512, 512)
            w = wup[:, :, :, :, cols].reshape(C, 512)
            t = jnp.dot(left, w, preferred_element_type=jnp.float32) + ub[:, cols]
            hid[:, cols] = gelu(t).astype(jnp.bfloat16)
        g = lax.div(b, 2)
        m0 = lax.rem(b, 2) * PER_BATCH
        h = hid[...]
        for n in range(2):
            cols = pl.ds(n * 512, 512)
            w = wdn[:, :, :, :, cols].reshape(HID, 512)
            t = jnp.dot(h, w, preferred_element_type=jnp.float32) + bd[:, cols]
            t = t.reshape(PER_BATCH, RING, 512)
            s = out[pl.ds(m0, PER_BATCH), g, :, cols].astype(jnp.float32)
            out[pl.ds(m0, PER_BATCH), g, :, cols] = (s + t).astype(jnp.bfloat16)
        return carry

    lax.fori_loop(0, 2 * PER_BATCH, cells, 0)

    rc(up_x(0), up_x(3), xs.at[0], xr.at[0], xdev(1)).wait_recv()
    send(rc(up_x(3), up_x(3), xs.at[4], xr.at[4], xdev(1)))
    send(rc(up_x(3), up_x(3), cs.at[0, 3], cr.at[0, 3], sib))
    rc(up_x(0), up_x(1), xs.at[1], xr.at[1], xdev(3)).wait_recv()
    send(rc(up_x(1), up_x(1), cs.at[0, 1], cr.at[0, 1], sib))
    rc(dn_x(0), dn_x(1), xs.at[3], xr.at[3], xdev(3)).wait_recv()
    send(rc(dn_x(1), dn_x(1), xs.at[5], xr.at[5], xdev(3)))
    send(rc(dn_x(1), dn_x(1), cs.at[1, 1], cr.at[1, 1], sib))
    rc(dn_x(0), dn_x(3), xs.at[2], xr.at[2], xdev(1)).wait_recv()
    send(rc(dn_x(3), dn_x(3), cs.at[1, 3], cr.at[1, 3], sib))

    lax.fori_loop(2 * PER_BATCH, 3 * PER_BATCH, cells, 0)

    rc(up_x(0), up_x(2), xs.at[4], xr.at[4], xdev(1)).wait_recv()
    send(rc(up_x(2), up_x(2), cs.at[0, 2], cr.at[0, 2], sib))
    rc(dn_x(0), dn_x(2), xs.at[5], xr.at[5], xdev(3)).wait_recv()
    send(rc(dn_x(2), dn_x(2), cs.at[1, 2], cr.at[1, 2], sib))
    for k in range(4):
        rc(up_x(k), up_x(k, sib_core), cs.at[0, k], cr.at[0, k], sib).wait_recv()
        rc(dn_x(k), dn_x(k, sib_core), cs.at[1, k], cr.at[1, k], sib).wait_recv()

    def step(b, carry):
        @pl.when(b >= 3)
        def _():
            lax.fori_loop(b * PER_BATCH, (b + 1) * PER_BATCH, cells, 0)

        return mlp(b, carry)

    lax.fori_loop(0, BATCHES, step, 0)

    for desc in waits:
        desc.wait_send()

    def end_halo(u, carry):
        a, b = halo(u)
        a.wait_send()
        b.wait_send()
        return carry

    lax.fori_loop(0, UNITS, end_halo, 0)


def shards(analysis, owner, noise, depth_weight, depth_bias, norm_gain, up_weight, up_bias, down_weight, down_bias):
    shape = noise.shape
    any_space = pl.BlockSpec(memory_space=pl.ANY)
    vmem = pl.BlockSpec(memory_space=pltpu.VMEM)
    dma = pltpu.SemaphoreType.DMA
    bf, f32 = jnp.bfloat16, jnp.float32
    result = pl.pallas_call(
        kernel,
        out_shape=jax.ShapeDtypeStruct((MEM, GROUPS, RING, C), bf),
        in_specs=[
            pl.BlockSpec(memory_space=pltpu.SMEM), any_space, any_space, vmem, vmem, vmem,
            any_space, vmem, any_space, vmem,
        ],
        out_specs=vmem,
        scratch_shapes=[
            pltpu.VMEM((MEM, GROUPS, RING, C), bf),
            pltpu.VMEM((UNITS, RING, C), bf),
            pltpu.VMEM((UNITS, RING, C), bf),
            pltpu.VMEM((UNITS * RING, C), bf),
            pltpu.VMEM((2, 8, 2, 32, HID), bf),
            pltpu.VMEM((2, 8, 2, 64, C), bf),
            pltpu.VMEM((3, GROUPS * RING, C), f32),
            pltpu.VMEM((2, GROUPS * RING, HALF), f32),
            pltpu.VMEM((GROUPS * RING, HALF), f32),
            pltpu.VMEM((4, SLICE, HALF), f32),
            pltpu.VMEM((2, SLICE, HALF), f32),
            pltpu.VMEM((RING, C), f32),
            pltpu.VMEM((ROWS, HID), bf),
            dma((2, UNITS)), dma((2, UNITS)),
            dma((2, 7)), dma((2, 7)),
            dma((6,)), dma((6,)),
            dma((6,)), dma((6,)),
            dma((2, 4)), dma((2, 4)),
            dma((19,)), dma((19,)),
            dma((4,)),
        ],
        compiler_params=pltpu.CompilerParams(
            collective_id=0, has_side_effects=True, vmem_limit_bytes=50 * 1024 * 1024
        ),
        name="block",
    )(
        owner,
        analysis.reshape(GROUPS * RING, C),
        noise.reshape(MEM, GROUPS, RING, C),
        depth_weight.reshape(9, C),
        depth_bias.reshape(1, C),
        norm_gain.reshape(1, C),
        up_weight.reshape(2, 32, HID),
        up_bias.reshape(1, HID),
        down_weight.reshape(2, 64, C),
        down_bias.reshape(1, C),
    )
    return result.reshape(shape)


def solution(mesh):
    placed = (
        P("member", None, "fsdp", None, None),
        P(),
        P("member", None, "fsdp", None, None),
        P(),
        P(),
        P(),
        P("fsdp", None),
        P(),
        P("fsdp", None),
        P(),
    )
    return jax.shard_map(
        shards,
        mesh=mesh,
        in_specs=placed,
        out_specs=P("member", None, "fsdp", None, None),
        check_vma=False,
    )
```

time: 350 us -> 179 us (0.51)
  waiting for transfers between devices: 196 us -> 0 us
  Pallas kernels: 0 us -> 167 us
  local copies, waits for them, and re-layouts: 72.9 us -> 10.7 us
  other arithmetic: 39 us -> 0 us
  matrix products: 19.6 us -> 0 us
  between operations: 15.8 us -> 0.68 us
  starting transfers between devices: 5.44 us -> 0 us
    pallas_call x0 -> x1, Pallas kernels: none -> 167 us  [shards(): pl.pallas_call(kernel, out_shape=jax.ShapeDtypeStruct((MEM, GROUPS, RING,...]
    psum x1 -> x0, waiting for transfers between devices: 129 us -> none  [from_root(): return lax.psum(jnp.where(mine, shard, jnp.zeros_like(shard)), axis)]
    ppermute x2 -> x0, waiting for transfers between devices: 66.4 us -> none  [the longest x1 66.4 us: padded_2(): lax.ppermute(tail, axis, [(i, (i + 1) % count) for i in range(count)])]
    gather x6 -> x0, local copies, waits for them, and re-layouts: 46.8 us -> none  [the longest x2 19.1 us: shards(): rows[:, right_table][:, :, :, 0:1]]
    dot_general x1 -> x0, matrix products: 19.6 us -> none  [shards(): jnp.dot(columns, lax.all_gather(down_weight, 'fsdp', axis=0, tiled=True),...]
    reduce_sum x2 -> x0, other arithmetic: 18.9 us -> none  [the longest x1 18.1 us: shards(): mean = jnp.mean(conv, axis=-1, keepdims=True)]
    unnamed x20 -> x15, local copies, waits for them, and re-layouts: 0.04 us -> 9.91 us
    concatenate x1 -> x0, local copies, waits for them, and re-layouts: 9.79 us -> none  [shards(): rows = jnp.concatenate([lower_rim, start, upper_rim], axis=2)]
  transfers between devices with their start and end apart: 5 -> 0, of which waited for: 2 -> 0; matrix products, arithmetic and copies ran while one was open for 32% -> 0% of each run, Pallas kernels for 0% -> 0%
where the time goes in v1:
time: 179 us; the launch traced here: 178 us
  Pallas kernels  167 us (93%)
  local copies, waits for them, and re-layouts  10.7 us (6%)
    pallas_call x1, Pallas kernels, shards(): pl.pallas_call(kernel, out_shape=jax.ShapeDtypeStruct((MEM, GROUPS, RING,...  167 us
    unnamed x15, local copies, waits for them, and re-layouts  9.91 us

profile of v1, /device:TPU:1, one launch (start us, length us, event | category | flops | bytes accessed | tf_op | source)
XLA Modules:
  0.0 178.2 jit_solution(18234541066586193944)
XLA Ops:
  0.7 0.8 reshape.32.dw
  1.5 0.0 copy-start
  1.5 1.1 copy-done
  2.6 0.0 copy-start.1
  2.6 0.9 copy-done.1
  3.6 0.0 copy-start.2
  3.6 0.9 copy-done.2
  4.5 0.0 copy-start.3
  4.5 0.7 copy-done.3
  5.2 0.0 copy-start.4
  5.2 0.7 copy-done.4
  5.9 0.0 copy-start.5
  5.9 0.7 copy-done.5
  6.6 0.0 copy-start.6
  6.6 0.7 copy-done.6
  7.3 166.8 %block.1 = bf16[8,3,64,1024]{3,2,1,0:T(8,128)(2,1)} custom-call(s32[1]{0:T(128)S(6)} %copy.13.owner_ref, f32[192,1024]{1,0:T(8,128)S(1)} %bitcast.11, bf16[8,3,64,1024]{3,2,1,0:T(8,128)(2,1)} %bitcast.19, f32[9,1024]{1,0:T(8,128)S(1)} %reshape.32.dw, f32[1,1024]{1,0:T(1,128)S(1)} %bitcast.15, f32[1,1024]{1,0:T(1,128)S(1)} %bitcast.16, ...), custom_call_target="tpu_custom_call" | custom-call | tf_op jit(solution)/shard_map/block/pallas_call | solution.py:329
  174.1 4.1 %copy.14 = bf16[8,12,1,16,1024]{4,3,2,1,0:T(8,128)(2,1)} copy(bf16[8,12,1,16,1024]{4,3,2,1,0:T(8,128)(2,1)} %bitcast.18) | data formatting | bytes 6291456
Async XLA Ops:
  1.5 1.1 copy-start
  2.6 0.9 copy-start.1
  3.6 0.9 copy-start.2
  4.5 0.7 copy-start.3
  5.2 0.7 copy-start.4
  5.9 0.7 copy-start.5
  6.6 0.7 copy-start.6
